TPU v7x, 32 devices: a whole 2x2x4 slice. The times are simulated.
32 devices in a mesh: section: 4 (over z), expert: 8 (over y, x, core).
Axes of the slice: x: 2, y: 2, z: 4, core: 2. Of those that a mesh axis runs over, the one named last changes fastest.
Arguments:
- features: bfloat16 [2, 512, 2048], P(None, 'expert'), may hold values from -6 to 6
- labels: int32 [2, 512], P(None, 'expert'), may hold values 0 or 1
- routes: int32 [4, 2, 512, 1], P('section', None, 'expert'), may hold values from 0 to 7; in each aligned block of 64 rows (0 to 63, 64 to 127, ..., all dimensions but the last counted through in order) at most 12 rows name the same one
- route_gates: float32 [4, 2, 512], P('section', None, 'expert'), may hold values from 0.25 to 1
- gate_weight: bfloat16 [4, 8, 2048, 256], P('section', 'expert'), may hold values from -0.125 to 0.125
- up_weight: bfloat16 [4, 8, 2048, 256], P('section', 'expert'), may hold values from -0.125 to 0.125
- down_weight: bfloat16 [4, 8, 256, 2048], P('section', 'expert'), may hold values from -0.375 to 0.375
- lowrank_in: bfloat16 [4, 2048, 128], P('section'), may hold values from -0.125 to 0.125
- lowrank_out: bfloat16 [4, 128, 2048], P('section'), may hold values from -0.5 to 0.5
- head_weight: float32 [2048], replicated, may hold values from -0.5 to 0.5
Outputs:
- grad_gate: float32 [4, 8, 2048, 256], P('section', 'expert')
- grad_up: float32 [4, 8, 2048, 256], P('section', 'expert')
- grad_down: float32 [4, 8, 256, 2048], P('section', 'expert')
- grad_lowrank_in: float32 [4, 2048, 128], P('section', 'expert')
- grad_lowrank_out: float32 [4, 128, 2048], P('section', None, 'expert')
Inputs may be any that keep to these rules, and one draw needn't show every extreme that they name: `routes`: in each layer and micro-batch the 64 rows of one device name one expert at most 12 times, and 12 is reached in every draw.
All inputs are finite; a program needn't handle non-finite values. No bound on the sum of `labels` on one device may be relied on, other than what follows from the above.
Results may differ from a plain program's by a relative error of at most 0.04.
Values may be sent and summed in bfloat16 or wider, within the bound.
A program may use at most 128 MiB of HBM per device.

v0:
```python
import functools

import jax
import jax.numpy as jnp
from jax import lax
from jax.experimental import pallas as pl
from jax.experimental.pallas import tpu as pltpu
from jax.sharding import PartitionSpec as P

epsilon = 1e-06
MESH = pl.DeviceIdType.MESH
f32, bf16 = jnp.float32, jnp.bfloat16
TILE = 16
NN = (((1,), (0,)), ((), ()))
NT = (((1,), (1,)), ((), ()))
TN = (((0,), (0,)), ((), ()))


def mm(left, right, dims=NN):
    return lax.dot_general(left, right, dims, preferred_element_type=f32)


def rms_scale(widened):
    return lax.rsqrt(jnp.mean(widened * widened, axis=-1, keepdims=True) + epsilon)


def norm_back(widened, row_scale, grad_norm):
    inner_mean = jnp.mean(grad_norm * widened, axis=-1, keepdims=True)
    return row_scale * grad_norm - widened * (row_scale * row_scale * row_scale) * inner_mean


def sigmoid(values):
    return jax.nn.sigmoid(values)


def kernel(
    sections, experts, slot,
    feat, label, id_row, id_col, gates, gate_w, up_w, down_w, low, head,
    out_gate, out_up, out_down, out_low,
    h_in, h_out, g_in, scale, spread, gather, outgoing, slots, back, slot_grads,
    gate_act, gate_slope, hidden, grad_gate, grad_up,
    low_all, low_rows, low_grads, low_scale, low_act, low_slope, low_pre, parts, shares, share_in,
    stage, out_sem,
    x_send, x_recv, hop_send, hop_recv, lw_send, lw_recv, lb_send, lb_recv,
    p_send, p_recv, q_send, q_recv,
):
    micro, rows, width = feat.shape
    count = experts * slot
    piece = width // experts
    last = sections - 1
    sec, me = lax.axis_index("section"), lax.axis_index("expert")
    mine = pl.ds(pl.multiple_of(me * piece, piece), piece)

    barrier = pltpu.get_barrier_semaphore()

    @pl.loop(1, experts)
    def _(k):
        pl.semaphore_signal(
            barrier, inc=1, device_id=(sec, lax.rem(me + k, experts)), device_id_type=MESH
        )

    @pl.loop(1, sections)
    def _(k):
        pl.semaphore_signal(
            barrier, inc=1, device_id=(lax.rem(sec + k, sections), me), device_id_type=MESH
        )

    pl.semaphore_wait(barrier, experts + sections - 2)

    def low_copy(source):
        return pltpu.make_async_remote_copy(
            src_ref=low.at[:, mine, :], dst_ref=low_all.at[source, :, mine, :],
            send_sem=lw_send, recv_sem=lw_recv.at[source],
            device_id=(last, me), device_id_type=MESH,
        )

    def low_spread(peer, owner):
        part = pl.ds(pl.multiple_of(owner * piece, piece), piece)
        view = low_all.at[pl.ds(0, last), :, part, :]
        return pltpu.make_async_remote_copy(
            src_ref=view, dst_ref=view, send_sem=lb_send.at[peer], recv_sem=lb_recv.at[owner],
            device_id=(sec, peer), device_id_type=MESH,
        )

    def exchange(phase, m, peer, owner, target):
        return pltpu.make_async_remote_copy(
            src_ref=outgoing.at[m, peer], dst_ref=target.at[m, owner],
            send_sem=x_send.at[phase, m, peer], recv_sem=x_recv.at[phase, m, owner],
            device_id=(sec, peer), device_id_type=MESH,
        )

    def send_slots(phase, m, target):
        @pl.loop(1, experts)
        def _(k):
            exchange(phase, m, lax.rem(me + k, experts), me, target).start()

        target[m, me] = outgoing[m, me]

    def wait_slots(phase, m, target):
        @pl.loop(1, experts)
        def _(k):
            peer = lax.rem(me + k, experts)
            exchange(phase, m, peer, peer, target).wait_recv()

    def wait_sent(phase, m, target):
        @pl.loop(1, experts)
        def _(k):
            exchange(phase, m, lax.rem(me + k, experts), me, target).wait_send()

    def hop(way, m, source, target, to):
        return pltpu.make_async_remote_copy(
            src_ref=source.at[m], dst_ref=target.at[m],
            send_sem=hop_send.at[way, m], recv_sem=hop_recv.at[way, m],
            device_id=(to, me), device_id_type=MESH,
        )

    below = lax.rem(sec + 1, sections)
    above = lax.rem(sec + sections - 1, sections)

    @pl.when(sec < last)
    def _():
        low_copy(sec).start()

    for m in range(micro):
        ids_row, ids_col = id_row[m].astype(f32), id_col[m].astype(f32)
        same = jnp.where(ids_col == ids_row, 1.0, 0.0)
        first = lax.broadcasted_iota(jnp.int32, (rows, rows), 0)
        second = lax.broadcasted_iota(jnp.int32, (rows, rows), 1)
        rank_col = jnp.sum(jnp.where(second < first, same, 0.0), axis=1, keepdims=True)
        rank_row = jnp.sum(jnp.where(first < second, same, 0.0), axis=0, keepdims=True)
        grid_row = lax.broadcasted_iota(jnp.int32, (count, rows), 0).astype(f32)
        grid_col = lax.broadcasted_iota(jnp.int32, (rows, count), 1).astype(f32)
        spread[m] = jnp.where(grid_row == ids_row * slot + rank_row, 1.0, 0.0).astype(bf16)
        gather[m] = jnp.where(grid_col == ids_col * slot + rank_col, 1.0, 0.0).astype(bf16)

    @pl.when(sec == last)
    def _():
        @pl.loop(0, last)
        def _(source):
            low_copy(source).wait_recv()

        @pl.loop(1, experts)
        def _(k):
            low_spread(lax.rem(me + k, experts), me).start()

        low_all[last] = low[...]

    group = min(experts, 8)
    wide = group * slot

    def in_groups(run):
        if experts == group:
            run(pl.ds(0, group), pl.ds(0, wide))
        else:

            @pl.loop(0, experts // group)
            def _(turn):
                run(
                    pl.ds(pl.multiple_of(turn * group, group), group),
                    pl.ds(pl.multiple_of(turn * wide, wide), wide),
                )

    def place(m, values):
        def run(peers, lines):
            placed = mm(spread[m, lines], values).astype(bf16)
            outgoing[m, peers] = placed.reshape(group, slot, width)

        in_groups(run)

    for m in range(micro):
        @pl.when(sec == 0)
        def _():
            h_in[m] = feat[m]

        @pl.when(sec > 0)
        def _():
            hop(0, m, h_out, h_in, below).wait_recv()

        values = h_in[m].astype(f32)
        row_scale = rms_scale(values)
        scale[m] = row_scale
        place(m, (values * row_scale).astype(bf16))
        send_slots(0, m, slots)

    for m in range(micro):
        wait_slots(0, m, slots)
        wait_sent(0, m, slots)

        def serve(peers, lines):
            normed = slots[m, peers].reshape(wide, width)
            gate_pre = mm(normed, gate_w[...])
            up_pre = mm(normed, up_w[...])
            gate_sig = sigmoid(gate_pre)
            act = gate_pre * gate_sig
            inner = (act * up_pre).astype(bf16)
            served = mm(inner, down_w[...]).astype(bf16)
            outgoing[m, peers] = served.reshape(group, slot, width)
            gate_act[m, lines] = act
            hidden[m, lines] = inner
            gate_slope[m, lines] = up_pre * (gate_sig * (1.0 + gate_pre * (1.0 - gate_sig)))

        in_groups(serve)
        send_slots(1, m, back)

    for m in range(micro):
        wait_slots(1, m, back)
        picked = mm(gather[m], back[m].reshape(count, width))
        h_out[m] = (h_in[m].astype(f32) + gates[m] * picked).astype(bf16)

        @pl.when(sec < last)
        def _():
            hop(0, m, h_out, h_in, below).start()

    for m in range(micro):
        wait_sent(1, m, back)

        @pl.when(sec < last)
        def _():
            hop(0, m, h_out, h_in, below).wait_send()

    @pl.when(sec == last)
    def _():
        @pl.loop(1, experts)
        def _(k):
            peer = lax.rem(me + k, experts)
            low_spread(peer, peer).wait_recv()

        low_rows[last] = h_out[...].reshape(micro * rows, width)

        def forward(step, carry):
            layer = last - step
            values = low_rows[layer].astype(f32)
            row_scale = rms_scale(values)
            low_scale[layer] = row_scale
            inner_pre = mm((values * row_scale).astype(bf16), low_all[layer, 0])
            inner_sig = sigmoid(inner_pre)
            inner_act = (inner_pre * inner_sig).astype(bf16)
            low_act[layer] = inner_act
            low_slope[layer] = inner_sig * (1.0 + inner_pre * (1.0 - inner_sig))
            result = (values + mm(inner_act, low_all[layer, 1], NT)).astype(bf16)

            @pl.when(layer > 0)
            def _():
                low_rows[layer - 1] = result

            @pl.when(layer == 0)
            def _():
                low_grads[0] = result

            return carry

        lax.fori_loop(0, sections, forward, 0)
        values = low_grads[0].astype(f32)
        row_scale = rms_scale(values)
        logits = row_scale * jnp.sum(values * head[...], axis=1, keepdims=True)
        grad_logit = sigmoid(logits) - label[...].astype(f32)
        low_grads[0] = norm_back(values, row_scale, grad_logit * head[...]).astype(bf16)

        def backward(layer, carry):
            values = low_rows[layer].astype(f32)
            row_scale = low_scale[layer]
            grads = low_grads[layer]
            grad_pre = (mm(grads, low_all[layer, 1]) * low_slope[layer]).astype(bf16)
            low_pre[layer] = grad_pre
            grad_norm = mm(grad_pre, low_all[layer, 0], NT)
            result = (grads.astype(f32) + norm_back(values, row_scale, grad_norm)).astype(bf16)

            @pl.when(layer < last)
            def _():
                low_grads[layer + 1] = result

            @pl.when(layer == last)
            def _():
                g_in[...] = result.reshape(micro, rows, width)

            return carry

        lax.fori_loop(0, sections, backward, 0)

    for m in range(micro):
        @pl.when(sec < last)
        def _():
            hop(1, m, h_out, g_in, above).wait_recv()

        place(m, (gates[m] * g_in[m].astype(f32)).astype(bf16))
        send_slots(2, m, slot_grads)

    for m in range(micro):
        wait_slots(2, m, slot_grads)
        wait_sent(2, m, slot_grads)

        def slope(peers, lines):
            grad_hidden = mm(slot_grads[m, peers].reshape(wide, width), down_w[...], NT)
            grad_gate[m, lines] = (grad_hidden * gate_slope[m, lines]).astype(bf16)
            grad_up[m, lines] = (grad_hidden * gate_act[m, lines]).astype(bf16)

        in_groups(slope)

        @pl.when(sec > 0)
        def _():
            def answer(peers, lines):
                grad_slots = mm(grad_gate[m, lines], gate_w[...], NT) + mm(
                    grad_up[m, lines], up_w[...], NT
                )
                outgoing[m, peers] = grad_slots.astype(bf16).reshape(group, slot, width)

            in_groups(answer)
            send_slots(3, m, back)

    @pl.when(sec > 0)
    def _():
        for m in range(micro):
            wait_slots(3, m, back)
            picked = mm(gather[m], back[m].reshape(count, width))
            h_out[m] = (
                g_in[m].astype(f32) + norm_back(h_in[m].astype(f32), scale[m], picked)
            ).astype(bf16)
            hop(1, m, h_out, g_in, above).start()

        for m in range(micro):
            wait_sent(3, m, back)

    def share_copy(peer, owner):
        part = pl.ds(pl.multiple_of(peer * piece, piece), piece)
        return pltpu.make_async_remote_copy(
            src_ref=low_all.at[:, :, part, :], dst_ref=parts.at[owner],
            send_sem=p_send.at[peer], recv_sem=p_recv.at[owner],
            device_id=(sec, peer), device_id_type=MESH,
        )

    def share_out(section):
        return pltpu.make_async_remote_copy(
            src_ref=shares.at[section], dst_ref=share_in, send_sem=q_send.at[section],
            recv_sem=q_recv, device_id=(section, me), device_id_type=MESH,
        )

    @pl.when(sec == last)
    def _():
        @pl.loop(1, experts)
        def _(k):
            low_spread(lax.rem(me + k, experts), me).wait_send()

        def products(layer, carry):
            normed = (low_rows[layer].astype(f32) * low_scale[layer]).astype(bf16)
            low_all[layer, 0] = mm(normed, low_pre[layer], TN).astype(bf16)
            low_all[layer, 1] = mm(low_grads[layer], low_act[layer], TN).astype(bf16)
            return carry

        lax.fori_loop(0, sections, products, 0)

        @pl.loop(1, experts)
        def _(k):
            share_copy(lax.rem(me + k, experts), me).start()

    flat = micro * count
    step = stage.shape[-1]
    chunks = width // step

    def writes(chunk):
        cols = pl.ds(pl.multiple_of(chunk * step, step), step)
        at = lax.rem(chunk, 2)
        targets = (out_gate.at[cols, :], out_up.at[cols, :], out_down.at[:, cols])
        return [
            pltpu.make_async_copy(stage.at[at, kind], target, out_sem.at[at, kind])
            for kind, target in enumerate(targets)
        ]

    @pl.loop(0, chunks)
    def _(chunk):
        @pl.when(chunk >= 2)
        def _():
            for copy in writes(chunk - 2):
                copy.wait()

        cols = pl.ds(pl.multiple_of(chunk * step, step), step)
        at = lax.rem(chunk, 2)
        normed = slots[:, :, :, cols].reshape(flat, step)
        grads = slot_grads[:, :, :, cols].reshape(flat, step)
        stage[at, 0] = mm(normed, grad_gate[...].reshape(flat, -1), TN)
        stage[at, 1] = mm(normed, grad_up[...].reshape(flat, -1), TN)
        stage[at, 2] = mm(hidden[...].reshape(flat, -1), grads, TN)
        for copy in writes(chunk):
            copy.start()

    for chunk in range(max(0, chunks - 2), chunks):
        for copy in writes(chunk):
            copy.wait()

    @pl.when(sec == last)
    def _():
        @pl.loop(1, experts)
        def _(k):
            peer = lax.rem(me + k, experts)
            share_copy(peer, peer).wait_recv()

        def total(layer, carry):
            def add(k, acc):
                return acc + parts[lax.rem(me + k, experts), layer].astype(f32)

            acc = lax.fori_loop(1, experts, add, low_all[layer, :, mine, :].astype(f32))
            shares[layer] = acc.astype(bf16)
            return carry

        lax.fori_loop(0, sections, total, 0)

        @pl.loop(0, last)
        def _(section):
            share_out(section).start()

        out_low[...] = shares[last].astype(f32)

        @pl.loop(0, last)
        def _(section):
            share_out(section).wait_send()

        @pl.loop(1, experts)
        def _(k):
            share_copy(lax.rem(me + k, experts), me).wait_send()

    @pl.when(sec < last)
    def _():
        low_copy(sec).wait_send()
        share_out(last).wait_recv()
        out_low[...] = share_in[...].astype(f32)

    @pl.when(sec > 0)
    def _():
        for m in range(micro):
            hop(1, m, h_out, g_in, above).wait_send()


def local(
    sections, experts,
    features, labels, routes, route_gates, gate_weight, up_weight, down_weight,
    lowrank_in, lowrank_out, head_weight,
):
    micro, rows, width = features.shape
    hidden_width, rank = gate_weight.shape[-1], lowrank_in.shape[-1]
    capacity = min(rows, max(2, 3 * rows // (2 * experts)))
    slot = -(-capacity // TILE) * TILE
    count, piece, flat = experts * slot, width // experts, micro * rows
    low = jnp.stack([lowrank_in[0], lowrank_out[0].T])
    ids = routes.reshape(micro, rows)
    vmem = pl.BlockSpec(memory_space=pltpu.VMEM)
    dma = pltpu.SemaphoreType.DMA
    buffer = pltpu.VMEM((micro, experts, slot, width), bf16)
    row_buffer = pltpu.VMEM((micro, rows, width), bf16)
    inner = lambda kind: pltpu.VMEM((micro, count, hidden_width), kind)
    out = pl.pallas_call(
        functools.partial(kernel, sections, experts, slot),
        out_shape=(
            jax.ShapeDtypeStruct((width, hidden_width), f32),
            jax.ShapeDtypeStruct((width, hidden_width), f32),
            jax.ShapeDtypeStruct((hidden_width, width), f32),
            jax.ShapeDtypeStruct((2, piece, rank), f32),
        ),
        in_specs=[vmem] * 10,
        out_specs=(pl.BlockSpec(memory_space=pl.ANY),) * 3 + (vmem,),
        scratch_shapes=[
            row_buffer, row_buffer, row_buffer,
            pltpu.VMEM((micro, rows, 1), f32),
            pltpu.VMEM((micro, count, rows), bf16),
            pltpu.VMEM((micro, rows, count), bf16),
            buffer, buffer, buffer, buffer,
            inner(f32), inner(f32), inner(bf16), inner(bf16), inner(bf16),
            pltpu.VMEM((sections, 2, width, rank), bf16),
            pltpu.VMEM((sections, flat, width), bf16),
            pltpu.VMEM((sections, flat, width), bf16),
            pltpu.VMEM((sections, flat, 1), f32),
            pltpu.VMEM((sections, flat, rank), bf16),
            pltpu.VMEM((sections, flat, rank), f32),
            pltpu.VMEM((sections, flat, rank), bf16),
            pltpu.VMEM((experts, sections, 2, piece, rank), bf16),
            pltpu.VMEM((sections, 2, piece, rank), bf16),
            pltpu.VMEM((2, piece, rank), bf16),
            pltpu.VMEM((2, 3, hidden_width, hidden_width), f32), dma((2, 3)),
            dma((4, micro, experts)), dma((4, micro, experts)),
            dma((2, micro)), dma((2, micro)),
            dma, dma((sections,)),
            dma((experts,)), dma((experts,)),
            dma((experts,)), dma((experts,)),
            dma((sections,)), dma,
        ],
        compiler_params=pltpu.CompilerParams(
            collective_id=0, has_side_effects=True, vmem_limit_bytes=60 * 1024 * 1024
        ),
    )(
        features, labels.reshape(flat, 1), ids[:, None, :], ids[:, :, None],
        route_gates.reshape(micro, rows, 1), gate_weight[0, 0], up_weight[0, 0],
        down_weight[0, 0], low, head_weight[None, :],
    )
    return (
        out[0][None, None], out[1][None, None], out[2][None, None], out[3][0][None],
        out[3][1].T[None],
    )


def solution(mesh):
    return jax.shard_map(
        functools.partial(local, mesh.shape["section"], mesh.shape["expert"]),
        mesh=mesh,
        in_specs=(
            P(None, "expert", None),
            P(None, "expert"),
            P("section", None, "expert", None),
            P("section", None, "expert"),
            P("section", "expert", None, None),
            P("section", "expert", None, None),
            P("section", "expert", None, None),
            P("section", None, None),
            P("section", None, None),
            P(),
        ),
        out_specs=(
            P("section", "expert", None, None),
            P("section", "expert", None, None),
            P("section", "expert", None, None),
            P("section", "expert", None),
            P("section", None, "expert"),
        ),
        check_vma=False,
    )
```

profile of v0, /device:TPU:1, one launch (start us, length us, event | category | flops | bytes accessed | tf_op | source)
XLA Modules:
  0.0 242.3 jit_solution(12946962140043785662)
XLA Ops:
  0.6 1.4 reshape.18.label
  2.1 1.4 copy.19.gates
  3.5 1.4 copy.18.id_col
  4.9 1.3 copy.15
  6.2 2.1 pad_maximum_fusion.low
  8.3 224.7 %shard_map.137 = (f32[2048,256]{1,0:T(8,128)}, f32[2048,256]{1,0:T(8,128)}, f32[256,2048]{1,0:T(8,128)}, f32[2,256,128]{2,1,0:T(8,128)}) custom-call(bf16[2,64,2048]{2,1,0:T(8,128)(2,1)} %feat.1, s32[128,1]{1,0:T(8,128)} %reshape.18.label, s32[2,1,64]{2,1,0:T(1,128)} %bitcast.32, s32[2,64,1]{2,1,0:T(8,128)} %copy.18.id_col, f32[2,64,1]{2,1,0:T(8,128)} %copy.19.gates, ...), custom_call_target="tpu_custom_call" | custom-call | tf_op jit(solution)/shard_map/pallas_call | solution.py:449
  233.1 1.6 slice_bitcast_fusion
  234.7 0.8 copy.20
  235.5 0.0 copy-start.1
  235.5 3.2 %copy.24 = f32[1,1,2048,256]{3,2,1,0:T(8,128)} copy(f32[1,1,2048,256]{3,2,1,0:T(8,128)} %bitcast.25) | data formatting | bytes 4194304
  238.7 0.0 copy-done.1
  238.7 0.0 copy-start
  238.7 1.3 copy.25
  240.0 1.0 copy-done
  241.0 1.3 copy.26
Async XLA Ops:
  235.5 3.2 %copy-start.1 = (f32[2048,256]{1,0:T(8,128)S(1)}, f32[2048,256]{1,0:T(8,128)}, u32[]{:S(2)}) copy-start(f32[2048,256]{1,0:T(8,128)} %get-tuple-element.10) | copy-start | bytes 6291460
  238.7 2.3 copy-start
where the time goes:
time: 243 us; the launch traced here: 242 us
  Pallas kernels  225 us (93%)
  local copies, waits for them, and re-layouts  14.8 us (6%)
    pallas_call x1, Pallas kernels, local(): pl.pallas_call(functools.partial(kernel, sections, experts, slot), out_sh...  225 us
    unnamed x9, local copies, waits for them, and re-layouts  8.93 us

commit v1 on v0

--- a/solution.py
+++ b/solution.py
@@ -35,12 +35,11 @@
 
 def kernel(
     sections, experts, slot,
-    feat, label, id_row, id_col, gates, gate_w, up_w, down_w, low, head,
-    out_gate, out_up, out_down, out_low,
-    h_in, h_out, g_in, scale, spread, gather, outgoing, slots, back, slot_grads,
-    gate_act, gate_slope, hidden, grad_gate, grad_up,
-    low_all, low_rows, low_grads, low_scale, low_act, low_slope, low_pre, parts, shares, share_in,
-    stage, out_sem,
+    feat, label, ids, gate_row, gate_w, up_w, down_w, low_in, low_out, head,
+    slots, slot_grads, hidden, grad_gate, grad_up, share_in,
+    h_in, h_out, g_in, scale, gates, spread, gather, outgoing, back,
+    gate_act, gate_slope,
+    low, low_all, low_rows, low_grads, low_scale, low_act, low_slope, low_pre, parts, shares,
     x_send, x_recv, hop_send, hop_recv, lw_send, lw_recv, lb_send, lb_recv,
     p_send, p_recv, q_send, q_recv,
 ):
@@ -117,21 +116,43 @@
     below = lax.rem(sec + 1, sections)
     above = lax.rem(sec + sections - 1, sections)
 
-    @pl.when(sec < last)
-    def _():
-        low_copy(sec).start()
-
-    for m in range(micro):
-        ids_row, ids_col = id_row[m].astype(f32), id_col[m].astype(f32)
+    def eye(size):
+        first = lax.broadcasted_iota(jnp.int32, (size, size), 0)
+        second = lax.broadcasted_iota(jnp.int32, (size, size), 1)
+        return first, second
+
+    def column(values):
+        first, second = eye(values.shape[1])
+        return jnp.sum(jnp.where(first == second, values, 0.0), axis=1, keepdims=True)
+
+    def prepare_low():
+        first, second = eye(low_out.shape[0])
+        low[0] = low_in[...]
+        low[1] = mm(low_out[...], jnp.where(first == second, 1.0, 0.0).astype(bf16), TN).astype(bf16)
+
+        @pl.when(sec < last)
+        def _():
+            low_copy(sec).start()
+
+    @pl.when(sec > 0)
+    def _():
+        prepare_low()
+
+    def prepare_routes(m):
+        ids_row = ids[m].astype(f32)
+        ids_col = column(ids_row)
         same = jnp.where(ids_col == ids_row, 1.0, 0.0)
-        first = lax.broadcasted_iota(jnp.int32, (rows, rows), 0)
-        second = lax.broadcasted_iota(jnp.int32, (rows, rows), 1)
+        first, second = eye(rows)
         rank_col = jnp.sum(jnp.where(second < first, same, 0.0), axis=1, keepdims=True)
         rank_row = jnp.sum(jnp.where(first < second, same, 0.0), axis=0, keepdims=True)
         grid_row = lax.broadcasted_iota(jnp.int32, (count, rows), 0).astype(f32)
         grid_col = lax.broadcasted_iota(jnp.int32, (rows, count), 1).astype(f32)
         spread[m] = jnp.where(grid_row == ids_row * slot + rank_row, 1.0, 0.0).astype(bf16)
         gather[m] = jnp.where(grid_col == ids_col * slot + rank_col, 1.0, 0.0).astype(bf16)
+        gates[m] = column(gate_row[m])
+
+    for m in range(micro):
+        prepare_routes(m)
 
     @pl.when(sec == last)
     def _():
@@ -167,7 +188,7 @@
 
         in_groups(run)
 
-    for m in range(micro):
+    def send_forward(m):
         @pl.when(sec == 0)
         def _():
             h_in[m] = feat[m]
@@ -182,7 +203,7 @@
         place(m, (values * row_scale).astype(bf16))
         send_slots(0, m, slots)
 
-    for m in range(micro):
+    def serve_forward(m):
         wait_slots(0, m, slots)
         wait_sent(0, m, slots)
 
@@ -202,7 +223,7 @@
         in_groups(serve)
         send_slots(1, m, back)
 
-    for m in range(micro):
+    def end_forward(m):
         wait_slots(1, m, back)
         picked = mm(gather[m], back[m].reshape(count, width))
         h_out[m] = (h_in[m].astype(f32) + gates[m] * picked).astype(bf16)
@@ -211,81 +232,66 @@
         def _():
             hop(0, m, h_out, h_in, below).start()
 
-    for m in range(micro):
         wait_sent(1, m, back)
 
-        @pl.when(sec < last)
-        def _():
-            hop(0, m, h_out, h_in, below).wait_send()
-
-    @pl.when(sec == last)
-    def _():
-        @pl.loop(1, experts)
-        def _(k):
-            peer = lax.rem(me + k, experts)
-            low_spread(peer, peer).wait_recv()
-
-        low_rows[last] = h_out[...].reshape(micro * rows, width)
+    def low_layers(m):
+        low_rows[last, m] = h_out[m]
 
         def forward(step, carry):
             layer = last - step
-            values = low_rows[layer].astype(f32)
+            values = low_rows[layer, m].astype(f32)
             row_scale = rms_scale(values)
-            low_scale[layer] = row_scale
+            low_scale[layer, m] = row_scale
             inner_pre = mm((values * row_scale).astype(bf16), low_all[layer, 0])
             inner_sig = sigmoid(inner_pre)
             inner_act = (inner_pre * inner_sig).astype(bf16)
-            low_act[layer] = inner_act
-            low_slope[layer] = inner_sig * (1.0 + inner_pre * (1.0 - inner_sig))
+            low_act[layer, m] = inner_act
+            low_slope[layer, m] = inner_sig * (1.0 + inner_pre * (1.0 - inner_sig))
             result = (values + mm(inner_act, low_all[layer, 1], NT)).astype(bf16)
 
             @pl.when(layer > 0)
             def _():
-                low_rows[layer - 1] = result
+                low_rows[layer - 1, m] = result
 
             @pl.when(layer == 0)
             def _():
-                low_grads[0] = result
+                low_grads[0, m] = result
 
             return carry
 
         lax.fori_loop(0, sections, forward, 0)
-        values = low_grads[0].astype(f32)
+        values = low_grads[0, m].astype(f32)
         row_scale = rms_scale(values)
         logits = row_scale * jnp.sum(values * head[...], axis=1, keepdims=True)
-        grad_logit = sigmoid(logits) - label[...].astype(f32)
-        low_grads[0] = norm_back(values, row_scale, grad_logit * head[...]).astype(bf16)
+        grad_logit = sigmoid(logits) - column(label[m].astype(f32))
+        low_grads[0, m] = norm_back(values, row_scale, grad_logit * head[...]).astype(bf16)
 
         def backward(layer, carry):
-            values = low_rows[layer].astype(f32)
-            row_scale = low_scale[layer]
-            grads = low_grads[layer]
-            grad_pre = (mm(grads, low_all[layer, 1]) * low_slope[layer]).astype(bf16)
-            low_pre[layer] = grad_pre
+            values = low_rows[layer, m].astype(f32)
+            row_scale = low_scale[layer, m]
+            grads = low_grads[layer, m]
+            grad_pre = (mm(grads, low_all[layer, 1]) * low_slope[layer, m]).astype(bf16)
+            low_pre[layer, m] = grad_pre
             grad_norm = mm(grad_pre, low_all[layer, 0], NT)
             result = (grads.astype(f32) + norm_back(values, row_scale, grad_norm)).astype(bf16)
 
             @pl.when(layer < last)
             def _():
-                low_grads[layer + 1] = result
+                low_grads[layer + 1, m] = result
 
             @pl.when(layer == last)
             def _():
-                g_in[...] = result.reshape(micro, rows, width)
+                g_in[m] = result
 
             return carry
 
         lax.fori_loop(0, sections, backward, 0)
 
-    for m in range(micro):
-        @pl.when(sec < last)
-        def _():
-            hop(1, m, h_out, g_in, above).wait_recv()
-
+    def send_backward(m):
         place(m, (gates[m] * g_in[m].astype(f32)).astype(bf16))
         send_slots(2, m, slot_grads)
 
-    for m in range(micro):
+    def serve_backward(m):
         wait_slots(2, m, slot_grads)
         wait_sent(2, m, slot_grads)
 
@@ -307,18 +313,83 @@
             in_groups(answer)
             send_slots(3, m, back)
 
-    @pl.when(sec > 0)
-    def _():
-        for m in range(micro):
+    def end_backward(m):
+        @pl.when(sec > 0)
+        def _():
             wait_slots(3, m, back)
             picked = mm(gather[m], back[m].reshape(count, width))
+
+            @pl.when(sec < last)
+            def _():
+                hop(0, m, h_out, h_in, below).wait_send()
+
             h_out[m] = (
                 g_in[m].astype(f32) + norm_back(h_in[m].astype(f32), scale[m], picked)
             ).astype(bf16)
             hop(1, m, h_out, g_in, above).start()
-
+            wait_sent(3, m, back)
+
+        @pl.when(sec == 0)
+        def _():
+            hop(0, m, h_out, h_in, below).wait_send()
+
+    send_forward(0)
+
+    @pl.when(sec == 0)
+    def _():
+        prepare_low()
+
+    for m in range(micro):
+        if m:
+            send_forward(m)
+
+            @pl.when(sec == last)
+            def _():
+                if m == 1:
+                    @pl.loop(1, experts)
+                    def _(k):
+                        peer = lax.rem(me + k, experts)
+                        low_spread(peer, peer).wait_recv()
+
+                low_layers(m - 1)
+                send_backward(m - 1)
+
+        serve_forward(m)
+        if m:
+            @pl.when(sec == last)
+            def _():
+                serve_backward(m - 1)
+
+        end_forward(m)
+        if m > 1:
+            @pl.when(sec == last)
+            def _():
+                end_backward(m - 2)
+
+    final = micro - 1
+
+    @pl.when(sec == last)
+    def _():
+        if micro == 1:
+            @pl.loop(1, experts)
+            def _(k):
+                peer = lax.rem(me + k, experts)
+                low_spread(peer, peer).wait_recv()
+
+        low_layers(final)
+        send_backward(final)
+        if micro > 1:
+            end_backward(final - 1)
+        serve_backward(final)
+        end_backward(final)
+
+    @pl.when(sec < last)
+    def _():
         for m in range(micro):
-            wait_sent(3, m, back)
+            hop(1, m, h_out, g_in, above).wait_recv()
+            send_backward(m)
+            serve_backward(m)
+            end_backward(m)
 
     def share_copy(peer, owner):
         part = pl.ds(pl.multiple_of(peer * piece, piece), piece)
@@ -342,8 +413,12 @@
 
         def products(layer, carry):
             normed = (low_rows[layer].astype(f32) * low_scale[layer]).astype(bf16)
-            low_all[layer, 0] = mm(normed, low_pre[layer], TN).astype(bf16)
-            low_all[layer, 1] = mm(low_grads[layer], low_act[layer], TN).astype(bf16)
+            normed = normed.reshape(micro * rows, width)
+            grads = low_grads[layer].reshape(micro * rows, width)
+            pre = low_pre[layer].reshape(micro * rows, -1)
+            act = low_act[layer].reshape(micro * rows, -1)
+            low_all[layer, 0] = mm(normed, pre, TN).astype(bf16)
+            low_all[layer, 1] = mm(grads, act, TN).astype(bf16)
             return carry
 
         lax.fori_loop(0, sections, products, 0)
@@ -351,40 +426,6 @@
         @pl.loop(1, experts)
         def _(k):
             share_copy(lax.rem(me + k, experts), me).start()
-
-    flat = micro * count
-    step = stage.shape[-1]
-    chunks = width // step
-
-    def writes(chunk):
-        cols = pl.ds(pl.multiple_of(chunk * step, step), step)
-        at = lax.rem(chunk, 2)
-        targets = (out_gate.at[cols, :], out_up.at[cols, :], out_down.at[:, cols])
-        return [
-            pltpu.make_async_copy(stage.at[at, kind], target, out_sem.at[at, kind])
-            for kind, target in enumerate(targets)
-        ]
-
-    @pl.loop(0, chunks)
-    def _(chunk):
-        @pl.when(chunk >= 2)
-        def _():
-            for copy in writes(chunk - 2):
-                copy.wait()
-
-        cols = pl.ds(pl.multiple_of(chunk * step, step), step)
-        at = lax.rem(chunk, 2)
-        normed = slots[:, :, :, cols].reshape(flat, step)
-        grads = slot_grads[:, :, :, cols].reshape(flat, step)
-        stage[at, 0] = mm(normed, grad_gate[...].reshape(flat, -1), TN)
-        stage[at, 1] = mm(normed, grad_up[...].reshape(flat, -1), TN)
-        stage[at, 2] = mm(hidden[...].reshape(flat, -1), grads, TN)
-        for copy in writes(chunk):
-            copy.start()
-
-    for chunk in range(max(0, chunks - 2), chunks):
-        for copy in writes(chunk):
-            copy.wait()
 
     @pl.when(sec == last)
     def _():
@@ -407,7 +448,7 @@
         def _(section):
             share_out(section).start()
 
-        out_low[...] = shares[last].astype(f32)
+        share_in[...] = shares[last]
 
         @pl.loop(0, last)
         def _(section):
@@ -421,12 +462,29 @@
     def _():
         low_copy(sec).wait_send()
         share_out(last).wait_recv()
-        out_low[...] = share_in[...].astype(f32)
 
     @pl.when(sec > 0)
     def _():
         for m in range(micro):
             hop(1, m, h_out, g_in, above).wait_send()
+
+
+def products_kernel(
+    slots, slot_grads, hidden, grad_gate, grad_up, share,
+    out_gate, out_up, out_down, out_in, out_out,
+):
+    out_gate[...] = mm(slots[...], grad_gate[...], TN)
+    out_up[...] = mm(slots[...], grad_up[...], TN)
+    out_down[...] = mm(hidden[...], slot_grads[...], TN)
+
+    @pl.when(pl.program_id(0) == 0)
+    def _():
+        out_in[...] = share[0].astype(f32)
+        size = share.shape[2]
+        first = lax.broadcasted_iota(jnp.int32, (size, size), 0)
+        second = lax.broadcasted_iota(jnp.int32, (size, size), 1)
+        unit = jnp.where(first == second, 1.0, 0.0).astype(bf16)
+        out_out[...] = mm(unit, share[1], NT)
 
 
 def local(
@@ -435,45 +493,43 @@
     lowrank_in, lowrank_out, head_weight,
 ):
     micro, rows, width = features.shape
-    hidden_width, rank = gate_weight.shape[-1], lowrank_in.shape[-1]
+    inner_width, rank = gate_weight.shape[-1], lowrank_in.shape[-1]
     capacity = min(rows, max(2, 3 * rows // (2 * experts)))
     slot = -(-capacity // TILE) * TILE
-    count, piece, flat = experts * slot, width // experts, micro * rows
-    low = jnp.stack([lowrank_in[0], lowrank_out[0].T])
-    ids = routes.reshape(micro, rows)
+    count, piece = experts * slot, width // experts
+    flat = micro * count
     vmem = pl.BlockSpec(memory_space=pltpu.VMEM)
     dma = pltpu.SemaphoreType.DMA
     buffer = pltpu.VMEM((micro, experts, slot, width), bf16)
     row_buffer = pltpu.VMEM((micro, rows, width), bf16)
-    inner = lambda kind: pltpu.VMEM((micro, count, hidden_width), kind)
-    out = pl.pallas_call(
+    slot_shape = jax.ShapeDtypeStruct((micro, experts, slot, width), bf16)
+    inner_shape = jax.ShapeDtypeStruct((micro, count, inner_width), bf16)
+    inner = pltpu.VMEM((micro, count, inner_width), f32)
+    low_buffer = pltpu.VMEM((sections, micro, rows, width), bf16)
+    made = pl.pallas_call(
         functools.partial(kernel, sections, experts, slot),
         out_shape=(
-            jax.ShapeDtypeStruct((width, hidden_width), f32),
-            jax.ShapeDtypeStruct((width, hidden_width), f32),
-            jax.ShapeDtypeStruct((hidden_width, width), f32),
-            jax.ShapeDtypeStruct((2, piece, rank), f32),
+            slot_shape, slot_shape, inner_shape, inner_shape, inner_shape,
+            jax.ShapeDtypeStruct((2, piece, rank), bf16),
         ),
         in_specs=[vmem] * 10,
-        out_specs=(pl.BlockSpec(memory_space=pl.ANY),) * 3 + (vmem,),
+        out_specs=(vmem,) * 6,
         scratch_shapes=[
             row_buffer, row_buffer, row_buffer,
             pltpu.VMEM((micro, rows, 1), f32),
+            pltpu.VMEM((micro, rows, 1), f32),
             pltpu.VMEM((micro, count, rows), bf16),
             pltpu.VMEM((micro, rows, count), bf16),
-            buffer, buffer, buffer, buffer,
-            inner(f32), inner(f32), inner(bf16), inner(bf16), inner(bf16),
+            buffer, buffer, inner, inner,
+            pltpu.VMEM((2, width, rank), bf16),
             pltpu.VMEM((sections, 2, width, rank), bf16),
-            pltpu.VMEM((sections, flat, width), bf16),
-            pltpu.VMEM((sections, flat, width), bf16),
-            pltpu.VMEM((sections, flat, 1), f32),
-            pltpu.VMEM((sections, flat, rank), bf16),
-            pltpu.VMEM((sections, flat, rank), f32),
-            pltpu.VMEM((sections, flat, rank), bf16),
+            low_buffer, low_buffer,
+            pltpu.VMEM((sections, micro, rows, 1), f32),
+            pltpu.VMEM((sections, micro, rows, rank), bf16),
+            pltpu.VMEM((sections, micro, rows, rank), f32),
+            pltpu.VMEM((sections, micro, rows, rank), bf16),
             pltpu.VMEM((experts, sections, 2, piece, rank), bf16),
             pltpu.VMEM((sections, 2, piece, rank), bf16),
-            pltpu.VMEM((2, piece, rank), bf16),
-            pltpu.VMEM((2, 3, hidden_width, hidden_width), f32), dma((2, 3)),
             dma((4, micro, experts)), dma((4, micro, experts)),
             dma((2, micro)), dma((2, micro)),
             dma, dma((sections,)),
@@ -485,13 +541,43 @@
             collective_id=0, has_side_effects=True, vmem_limit_bytes=60 * 1024 * 1024
         ),
     )(
-        features, labels.reshape(flat, 1), ids[:, None, :], ids[:, :, None],
-        route_gates.reshape(micro, rows, 1), gate_weight[0, 0], up_weight[0, 0],
-        down_weight[0, 0], low, head_weight[None, :],
+        features, labels.reshape(micro, 1, rows), routes.reshape(micro, 1, rows),
+        route_gates.reshape(micro, 1, rows), gate_weight[0, 0], up_weight[0, 0],
+        down_weight[0, 0], lowrank_in[0], lowrank_out[0], head_weight[None, :],
+    )
+    slots, slot_grads, hidden, grad_gate, grad_up, share = made
+    step = min(width, 512)
+    wide = pl.BlockSpec((flat, step), lambda i: (0, i))
+    narrow = pl.BlockSpec((flat, inner_width), lambda i: (0, 0))
+    tall = pl.BlockSpec((step, inner_width), lambda i: (i, 0))
+    outs = pl.pallas_call(
+        products_kernel,
+        grid=(width // step,),
+        out_shape=(
+            jax.ShapeDtypeStruct((width, inner_width), f32),
+            jax.ShapeDtypeStruct((width, inner_width), f32),
+            jax.ShapeDtypeStruct((inner_width, width), f32),
+            jax.ShapeDtypeStruct((piece, rank), f32),
+            jax.ShapeDtypeStruct((rank, piece), f32),
+        ),
+        in_specs=[
+            wide, wide, narrow, narrow, narrow,
+            pl.BlockSpec((2, piece, rank), lambda i: (0, 0, 0)),
+        ],
+        out_specs=(
+            tall, tall, pl.BlockSpec((inner_width, step), lambda i: (0, i)),
+            pl.BlockSpec((piece, rank), lambda i: (0, 0)),
+            pl.BlockSpec((rank, piece), lambda i: (0, 0)),
+        ),
+        compiler_params=pltpu.CompilerParams(vmem_limit_bytes=32 * 1024 * 1024),
+    )(
+        slots.reshape(flat, width), slot_grads.reshape(flat, width),
+        hidden.reshape(flat, inner_width), grad_gate.reshape(flat, inner_width),
+        grad_up.reshape(flat, inner_width), share,
     )
     return (
-        out[0][None, None], out[1][None, None], out[2][None, None], out[3][0][None],
-        out[3][1].T[None],
+        outs[0][None, None], outs[1][None, None], outs[2][None, None], outs[3][None],
+        outs[4][None],
     )
 
 

time: 243 us -> 217 us (0.89)
  Pallas kernels: 225 us -> 210 us
  local copies, waits for them, and re-layouts: 14.8 us -> 6.06 us
    pallas_call x1, Pallas kernels: 225 us -> 206 us  [local(): pl.pallas_call(functools.partial(kernel, sections, experts, slot), out_sh...]
    pallas_call x0 -> x1, Pallas kernels: none -> 3.96 us  [local(): pl.pallas_call(products_kernel, grid=(width // step,), out_shape=(jax.Sha...]
    unnamed x9 -> x12, local copies, waits for them, and re-layouts: 8.93 us -> 6.06 us
    reshape x2 -> x0, local copies, waits for them, and re-layouts: 2.86 us -> none  [the longest x1 1.45 us: local(): labels.reshape(flat, 1)]
where the time goes in v1:
time: 217 us; the launch traced here: 216 us
  Pallas kernels  210 us (97%)
  local copies, waits for them, and re-layouts  6.06 us (3%)
    pallas_call x1, Pallas kernels, local(): pl.pallas_call(functools.partial(kernel, sections, experts, slot), out_sh...  206 us
    unnamed x12, local copies, waits for them, and re-layouts  6.06 us

profile of v1, /device:TPU:1, one launch (start us, length us, event | category | flops | bytes accessed | tf_op | source)
XLA Modules:
  0.0 216.3 jit_solution(8899122163577831541)
XLA Ops:
  0.6 205.7 %shard_map.137 = (bf16[2,8,16,2048]{3,2,1,0:T(8,128)(2,1)}, bf16[2,8,16,2048]{3,2,1,0:T(8,128)(2,1)}, bf16[2,128,256]{2,1,0:T(8,128)(2,1)}, bf16[2,128,256]{2,1,...) custom-call(bf16[2,64,2048]{2,1,0:T(8,128)(2,1)} %feat.1, s32[2,1,64]{2,1,0:T(1,128)} %bitcast.36, ...), custom_call_target="tpu_custom_call" | custom-call | tf_op jit(solution)/shard_map/pallas_call | solution.py:509
  206.3 0.0 copy-start
  206.3 1.2 copy-done
  207.5 0.0 copy-start.1
  207.6 1.2 copy-done.1
  208.8 0.0 copy-start.2
  208.8 0.9 copy-done.2
  209.7 0.0 copy-start.3
  209.7 0.9 copy-done.3
  210.6 0.0 copy-start.4
  210.6 0.9 copy-done.4
  211.5 0.0 copy-start.5
  211.5 0.9 copy-done.5
  212.4 4.0 %shard_map.138 = (f32[2048,256]{1,0:T(8,128)}, f32[2048,256]{1,0:T(8,128)}, f32[256,2048]{1,0:T(8,128)}, f32[256,128]{1,0:T(8,128)}, f32[128,256]{1,0:T(8,128)}) custom-call(bf16[256,2048]{1,0:T(8,128)(2,1)S(1)} %bitcast.25, bf16[256,2048]{1,0:T(8,128)(2,1)S(1)} %bitcast.26, bf16[256,256]{1,0:T(8,128)(2,1)S(1)} %bitcast.27, bf16[256,256]{1,0:T(8,128)(2,1)S(1)} %bitcast.28, ...), custom_call_target="tpu_custom_call" | custom-call | tf_op jit(solution)/shard_map/pallas_call | solution.py:553
Async XLA Ops:
  206.3 1.2 copy-start
  207.5 1.2 copy-start.1
  208.8 0.9 copy-start.2
  209.7 0.9 copy-start.3
  210.6 0.9 copy-start.4
  211.5 0.9 copy-start.5

commit v2 on v1

--- a/solution.py
+++ b/solution.py
@@ -11,6 +11,7 @@
 MESH = pl.DeviceIdType.MESH
 f32, bf16 = jnp.float32, jnp.bfloat16
 TILE = 16
+PIECES = 4
 NN = (((1,), (0,)), ((), ()))
 NT = (((1,), (1,)), ((), ()))
 TN = (((0,), (0,)), ((), ()))
@@ -24,6 +25,10 @@
     return lax.rsqrt(jnp.mean(widened * widened, axis=-1, keepdims=True) + epsilon)
 
 
+def columns_of(values, piece, at):
+    return values[:, at * piece : (at + 1) * piece]
+
+
 def norm_back(widened, row_scale, grad_norm):
     inner_mean = jnp.mean(grad_norm * widened, axis=-1, keepdims=True)
     return row_scale * grad_norm - widened * (row_scale * row_scale * row_scale) * inner_mean
@@ -36,8 +41,8 @@
 def kernel(
     sections, experts, slot,
     feat, label, ids, gate_row, gate_w, up_w, down_w, low_in, low_out, head,
-    slots, slot_grads, hidden, grad_gate, grad_up, share_in,
-    h_in, h_out, g_in, scale, gates, spread, gather, outgoing, back,
+    slots, slot_scale, slot_grads, hidden, grad_gate, grad_up, share_in,
+    h_in, h_out, g_in, gates, spread, gather, outgoing, back,
     gate_act, gate_slope,
     low, low_all, low_rows, low_grads, low_scale, low_act, low_slope, low_pre, parts, shares,
     x_send, x_recv, hop_send, hop_recv, lw_send, lw_recv, lb_send, lb_recv,
@@ -46,6 +51,7 @@
     micro, rows, width = feat.shape
     count = experts * slot
     piece = width // experts
+    part_width = width // PIECES
     last = sections - 1
     sec, me = lax.axis_index("section"), lax.axis_index("expert")
     mine = pl.ds(pl.multiple_of(me * piece, piece), piece)
@@ -81,35 +87,35 @@
             device_id=(sec, peer), device_id_type=MESH,
         )
 
-    def exchange(phase, m, peer, owner, target):
+    def exchange(phase, m, c, peer, owner, target):
         return pltpu.make_async_remote_copy(
-            src_ref=outgoing.at[m, peer], dst_ref=target.at[m, owner],
-            send_sem=x_send.at[phase, m, peer], recv_sem=x_recv.at[phase, m, owner],
+            src_ref=outgoing.at[m, c, peer], dst_ref=target.at[m, c, owner],
+            send_sem=x_send.at[phase, m, c, peer], recv_sem=x_recv.at[phase, m, c, owner],
             device_id=(sec, peer), device_id_type=MESH,
         )
 
-    def send_slots(phase, m, target):
-        @pl.loop(1, experts)
-        def _(k):
-            exchange(phase, m, lax.rem(me + k, experts), me, target).start()
-
-        target[m, me] = outgoing[m, me]
-
-    def wait_slots(phase, m, target):
+    def send_slots(phase, m, c, target):
+        @pl.loop(1, experts)
+        def _(k):
+            exchange(phase, m, c, lax.rem(me + k, experts), me, target).start()
+
+        target[m, c, me] = outgoing[m, c, me]
+
+    def wait_slots(phase, m, c, target):
         @pl.loop(1, experts)
         def _(k):
             peer = lax.rem(me + k, experts)
-            exchange(phase, m, peer, peer, target).wait_recv()
-
-    def wait_sent(phase, m, target):
-        @pl.loop(1, experts)
-        def _(k):
-            exchange(phase, m, lax.rem(me + k, experts), me, target).wait_send()
-
-    def hop(way, m, source, target, to):
+            exchange(phase, m, c, peer, peer, target).wait_recv()
+
+    def wait_sent(phase, m, c, target):
+        @pl.loop(1, experts)
+        def _(k):
+            exchange(phase, m, c, lax.rem(me + k, experts), me, target).wait_send()
+
+    def hop(way, m, c, source, target, to):
         return pltpu.make_async_remote_copy(
-            src_ref=source.at[m], dst_ref=target.at[m],
-            send_sem=hop_send.at[way, m], recv_sem=hop_recv.at[way, m],
+            src_ref=source.at[m, c], dst_ref=target.at[m, c],
+            send_sem=hop_send.at[way, m, c], recv_sem=hop_recv.at[way, m, c],
             device_id=(to, me), device_id_type=MESH,
         )
 
@@ -181,61 +187,82 @@
                     pl.ds(pl.multiple_of(turn * wide, wide), wide),
                 )
 
-    def place(m, values):
+    def place(m, c, values):
         def run(peers, lines):
             placed = mm(spread[m, lines], values).astype(bf16)
-            outgoing[m, peers] = placed.reshape(group, slot, width)
+            outgoing[m, c, peers] = placed.reshape(group, slot, part_width)
 
         in_groups(run)
 
+    def cols(c):
+        return pl.ds(c * part_width, part_width)
+
+    def lines_of(buffer, m, c, peers):
+        return buffer[m, c, peers].reshape(wide, part_width)
+
     def send_forward(m):
-        @pl.when(sec == 0)
-        def _():
-            h_in[m] = feat[m]
-
-        @pl.when(sec > 0)
-        def _():
-            hop(0, m, h_out, h_in, below).wait_recv()
-
-        values = h_in[m].astype(f32)
-        row_scale = rms_scale(values)
-        scale[m] = row_scale
-        place(m, (values * row_scale).astype(bf16))
-        send_slots(0, m, slots)
+        for c in range(PIECES):
+            @pl.when(sec == 0)
+            def _():
+                h_in[m, c] = feat[m, :, cols(c)]
+
+            @pl.when(sec > 0)
+            def _():
+                hop(0, m, c, h_out, h_in, below).wait_recv()
+
+            place(m, c, h_in[m, c])
+            send_slots(0, m, c, slots)
 
     def serve_forward(m):
-        wait_slots(0, m, slots)
-        wait_sent(0, m, slots)
-
-        def serve(peers, lines):
-            normed = slots[m, peers].reshape(wide, width)
-            gate_pre = mm(normed, gate_w[...])
-            up_pre = mm(normed, up_w[...])
+        for c in range(PIECES):
+            wait_slots(0, m, c, slots)
+
+        def inward(peers, lines):
+            total = 0.0
+            for c in range(PIECES):
+                values = lines_of(slots, m, c, peers).astype(f32)
+                total = total + jnp.sum(values * values, axis=-1, keepdims=True)
+            row_scale = lax.rsqrt(total / width + epsilon)
+            slot_scale[m, lines] = row_scale
+            gate_pre, up_pre = 0.0, 0.0
+            for c in range(PIECES):
+                values = lines_of(slots, m, c, peers).astype(f32)
+                normed = (values * row_scale).astype(bf16)
+                gate_pre = gate_pre + mm(normed, gate_w[cols(c), :])
+                up_pre = up_pre + mm(normed, up_w[cols(c), :])
             gate_sig = sigmoid(gate_pre)
             act = gate_pre * gate_sig
-            inner = (act * up_pre).astype(bf16)
-            served = mm(inner, down_w[...]).astype(bf16)
-            outgoing[m, peers] = served.reshape(group, slot, width)
             gate_act[m, lines] = act
-            hidden[m, lines] = inner
+            hidden[m, lines] = (act * up_pre).astype(bf16)
             gate_slope[m, lines] = up_pre * (gate_sig * (1.0 + gate_pre * (1.0 - gate_sig)))
 
-        in_groups(serve)
-        send_slots(1, m, back)
+        in_groups(inward)
+        for c in range(PIECES):
+            wait_sent(0, m, c, slots)
+
+            def outward(peers, lines):
+                served = mm(hidden[m, lines], down_w[:, cols(c)]).astype(bf16)
+                outgoing[m, c, peers] = served.reshape(group, slot, part_width)
+
+            in_groups(outward)
+            send_slots(1, m, c, back)
 
     def end_forward(m):
-        wait_slots(1, m, back)
-        picked = mm(gather[m], back[m].reshape(count, width))
-        h_out[m] = (h_in[m].astype(f32) + gates[m] * picked).astype(bf16)
-
-        @pl.when(sec < last)
-        def _():
-            hop(0, m, h_out, h_in, below).start()
-
-        wait_sent(1, m, back)
+        for c in range(PIECES):
+            wait_slots(1, m, c, back)
+            picked = mm(gather[m], back[m, c].reshape(count, part_width))
+            h_out[m, c] = (h_in[m, c].astype(f32) + gates[m] * picked).astype(bf16)
+
+            @pl.when(sec < last)
+            def _():
+                hop(0, m, c, h_out, h_in, below).start()
+
+        for c in range(PIECES):
+            wait_sent(1, m, c, back)
 
     def low_layers(m):
-        low_rows[last, m] = h_out[m]
+        for c in range(PIECES):
+            low_rows[last, m, :, cols(c)] = h_out[m, c]
 
         def forward(step, carry):
             layer = last - step
@@ -281,57 +308,81 @@
 
             @pl.when(layer == last)
             def _():
-                g_in[m] = result
+                for c in range(PIECES):
+                    g_in[m, c] = columns_of(result, part_width, c)
 
             return carry
 
         lax.fori_loop(0, sections, backward, 0)
 
     def send_backward(m):
-        place(m, (gates[m] * g_in[m].astype(f32)).astype(bf16))
-        send_slots(2, m, slot_grads)
+        for c in range(PIECES):
+            @pl.when(sec < last)
+            def _():
+                hop(1, m, c, h_out, g_in, above).wait_recv()
+
+            place(m, c, (gates[m] * g_in[m, c].astype(f32)).astype(bf16))
+            send_slots(2, m, c, slot_grads)
 
     def serve_backward(m):
-        wait_slots(2, m, slot_grads)
-        wait_sent(2, m, slot_grads)
+        for c in range(PIECES):
+            wait_slots(2, m, c, slot_grads)
 
         def slope(peers, lines):
-            grad_hidden = mm(slot_grads[m, peers].reshape(wide, width), down_w[...], NT)
+            grad_hidden = 0.0
+            for c in range(PIECES):
+                grads = lines_of(slot_grads, m, c, peers)
+                grad_hidden = grad_hidden + mm(grads, down_w[:, cols(c)], NT)
             grad_gate[m, lines] = (grad_hidden * gate_slope[m, lines]).astype(bf16)
             grad_up[m, lines] = (grad_hidden * gate_act[m, lines]).astype(bf16)
 
         in_groups(slope)
+        for c in range(PIECES):
+            wait_sent(2, m, c, slot_grads)
 
         @pl.when(sec > 0)
         def _():
             def answer(peers, lines):
-                grad_slots = mm(grad_gate[m, lines], gate_w[...], NT) + mm(
-                    grad_up[m, lines], up_w[...], NT
-                )
-                outgoing[m, peers] = grad_slots.astype(bf16).reshape(group, slot, width)
+                row_scale = slot_scale[m, lines]
+                products, total = [], 0.0
+                for c in range(PIECES):
+                    grads = mm(grad_gate[m, lines], gate_w[cols(c), :], NT) + mm(
+                        grad_up[m, lines], up_w[cols(c), :], NT
+                    )
+                    values = lines_of(slots, m, c, peers).astype(f32)
+                    total = total + jnp.sum(grads * values, axis=-1, keepdims=True)
+                    products.append(grads)
+                weight = row_scale * row_scale * row_scale * (total / width)
+                for c in range(PIECES):
+                    values = lines_of(slots, m, c, peers).astype(f32)
+                    result = (row_scale * products[c] - values * weight).astype(bf16)
+                    outgoing[m, c, peers] = result.reshape(group, slot, part_width)
 
             in_groups(answer)
-            send_slots(3, m, back)
+            for c in range(PIECES):
+                send_slots(3, m, c, back)
 
     def end_backward(m):
         @pl.when(sec > 0)
         def _():
-            wait_slots(3, m, back)
-            picked = mm(gather[m], back[m].reshape(count, width))
-
-            @pl.when(sec < last)
-            def _():
-                hop(0, m, h_out, h_in, below).wait_send()
-
-            h_out[m] = (
-                g_in[m].astype(f32) + norm_back(h_in[m].astype(f32), scale[m], picked)
-            ).astype(bf16)
-            hop(1, m, h_out, g_in, above).start()
-            wait_sent(3, m, back)
+            for c in range(PIECES):
+                wait_slots(3, m, c, back)
+                picked = mm(gather[m], back[m, c].reshape(count, part_width))
+
+                @pl.when(sec < last)
+                def _():
+                    hop(0, m, c, h_out, h_in, below).wait_send()
+
+                h_out[m, c] = (g_in[m, c].astype(f32) + picked).astype(bf16)
+                hop(1, m, c, h_out, g_in, above).start()
+
+            for c in range(PIECES):
+                wait_sent(3, m, c, back)
 
         @pl.when(sec == 0)
         def _():
-            hop(0, m, h_out, h_in, below).wait_send()
+            for c in range(PIECES):
+                hop(0, m, c, h_out, h_in, below).wait_send()
 
     send_forward(0)
 
@@ -386,7 +437,6 @@
     @pl.when(sec < last)
     def _():
         for m in range(micro):
-            hop(1, m, h_out, g_in, above).wait_recv()
             send_backward(m)
             serve_backward(m)
             end_backward(m)
@@ -466,16 +516,20 @@
     @pl.when(sec > 0)
     def _():
         for m in range(micro):
-            hop(1, m, h_out, g_in, above).wait_send()
+            for c in range(PIECES):
+                hop(1, m, c, h_out, g_in, above).wait_send()
 
 
 def products_kernel(
-    slots, slot_grads, hidden, grad_gate, grad_up, share,
+    slots, scale, slot_grads, hidden, grad_gate, grad_up, share,
     out_gate, out_up, out_down, out_in, out_out,
 ):
-    out_gate[...] = mm(slots[...], grad_gate[...], TN)
-    out_up[...] = mm(slots[...], grad_up[...], TN)
-    out_down[...] = mm(hidden[...], slot_grads[...], TN)
+    flat = hidden.shape[0]
+    values = slots[...].reshape(flat, -1).astype(f32)
+    normed = (values * scale[...].reshape(flat, 1)).astype(bf16)
+    out_gate[...] = mm(normed, grad_gate[...], TN)
+    out_up[...] = mm(normed, grad_up[...], TN)
+    out_down[...] = mm(hidden[...], slot_grads[...].reshape(flat, -1), TN)
 
     @pl.when(pl.program_id(0) == 0)
     def _():
@@ -500,23 +554,23 @@
     flat = micro * count
     vmem = pl.BlockSpec(memory_space=pltpu.VMEM)
     dma = pltpu.SemaphoreType.DMA
-    buffer = pltpu.VMEM((micro, experts, slot, width), bf16)
-    row_buffer = pltpu.VMEM((micro, rows, width), bf16)
-    slot_shape = jax.ShapeDtypeStruct((micro, experts, slot, width), bf16)
+    step = width // PIECES
+    buffer = pltpu.VMEM((micro, PIECES, experts, slot, step), bf16)
+    row_buffer = pltpu.VMEM((micro, PIECES, rows, step), bf16)
+    slot_shape = jax.ShapeDtypeStruct((micro, PIECES, experts, slot, step), bf16)
     inner_shape = jax.ShapeDtypeStruct((micro, count, inner_width), bf16)
     inner = pltpu.VMEM((micro, count, inner_width), f32)
     low_buffer = pltpu.VMEM((sections, micro, rows, width), bf16)
     made = pl.pallas_call(
         functools.partial(kernel, sections, experts, slot),
         out_shape=(
-            slot_shape, slot_shape, inner_shape, inner_shape, inner_shape,
+            slot_shape, jax.ShapeDtypeStruct((micro, count, 1), f32), slot_shape, inner_shape, inner_shape, inner_shape,
             jax.ShapeDtypeStruct((2, piece, rank), bf16),
         ),
         in_specs=[vmem] * 10,
-        out_specs=(vmem,) * 6,
+        out_specs=(vmem,) * 7,
         scratch_shapes=[
             row_buffer, row_buffer, row_buffer,
-            pltpu.VMEM((micro, rows, 1), f32),
             pltpu.VMEM((micro, rows, 1), f32),
             pltpu.VMEM((micro, count, rows), bf16),
             pltpu.VMEM((micro, rows, count), bf16),
@@ -530,8 +584,8 @@
             pltpu.VMEM((sections, micro, rows, rank), bf16),
             pltpu.VMEM((experts, sections, 2, piece, rank), bf16),
             pltpu.VMEM((sections, 2, piece, rank), bf16),
-            dma((4, micro, experts)), dma((4, micro, experts)),
-            dma((2, micro)), dma((2, micro)),
+            dma((4, micro, PIECES, experts)), dma((4, micro, PIECES, experts)),
+            dma((2, micro, PIECES)), dma((2, micro, PIECES)),
             dma, dma((sections,)),
             dma((experts,)), dma((experts,)),
             dma((experts,)), dma((experts,)),
@@ -545,14 +599,13 @@
         route_gates.reshape(micro, 1, rows), gate_weight[0, 0], up_weight[0, 0],
         down_weight[0, 0], lowrank_in[0], lowrank_out[0], head_weight[None, :],
     )
-    slots, slot_grads, hidden, grad_gate, grad_up, share = made
-    step = min(width, 512)
-    wide = pl.BlockSpec((flat, step), lambda i: (0, i))
+    slots, scale, slot_grads, hidden, grad_gate, grad_up, share = made
+    wide = pl.BlockSpec((micro, 1, count, step), lambda i: (0, i, 0, 0))
     narrow = pl.BlockSpec((flat, inner_width), lambda i: (0, 0))
     tall = pl.BlockSpec((step, inner_width), lambda i: (i, 0))
     outs = pl.pallas_call(
         products_kernel,
-        grid=(width // step,),
+        grid=(PIECES,),
         out_shape=(
             jax.ShapeDtypeStruct((width, inner_width), f32),
             jax.ShapeDtypeStruct((width, inner_width), f32),
@@ -561,7 +614,7 @@
             jax.ShapeDtypeStruct((rank, piece), f32),
         ),
         in_specs=[
-            wide, wide, narrow, narrow, narrow,
+            wide, pl.BlockSpec((micro, count, 1), lambda i: (0, 0, 0)), wide, narrow, narrow, narrow,
             pl.BlockSpec((2, piece, rank), lambda i: (0, 0, 0)),
         ],
         out_specs=(
@@ -569,9 +622,10 @@
             pl.BlockSpec((piece, rank), lambda i: (0, 0)),
             pl.BlockSpec((rank, piece), lambda i: (0, 0)),
         ),
-        compiler_params=pltpu.CompilerParams(vmem_limit_bytes=32 * 1024 * 1024),
+        compiler_params=pltpu.CompilerParams(vmem_limit_bytes=60 * 1024 * 1024),
     )(
-        slots.reshape(flat, width), slot_grads.reshape(flat, width),
+        slots.reshape(micro, PIECES, count, step), scale,
+        slot_grads.reshape(micro, PIECES, count, step),
         hidden.reshape(flat, inner_width), grad_gate.reshape(flat, inner_width),
         grad_up.reshape(flat, inner_width), share,
     )

time: 217 us -> 190 us (0.88)
  Pallas kernels: 210 us -> 189 us
  local copies, waits for them, and re-layouts: 6.06 us -> 0 us
    pallas_call x1, Pallas kernels: 206 us -> 183 us  [local(): pl.pallas_call(functools.partial(kernel, sections, experts, slot), out_sh...]
    unnamed x12 -> x0, local copies, waits for them, and re-layouts: 6.06 us -> none
where the time goes in v2:
time: 190 us
  Pallas kernels  189 us (99%)
    pallas_call x1, Pallas kernels, local(): pl.pallas_call(functools.partial(kernel, sections, experts, slot), out_sh...  183 us
    pallas_call x1, Pallas kernels, local(): pl.pallas_call(products_kernel, grid=(PIECES,), out_shape=(jax.ShapeDtype...  5.93 us

profile of v2, /device:TPU:1, one launch (start us, length us, event | category | flops | bytes accessed | tf_op | source)
XLA Modules:
  0.0 189.6 jit_solution(9399590617891261696)
XLA Ops:
  0.6 183.0 %shard_map.137 = (bf16[2,4,8,16,512]{4,3,2,1,0:T(8,128)(2,1)}, f32[2,128,1]{2,1,0:T(8,128)}, bf16[2,4,8,16,512]{4,3,2,1,0:T(8,128)(2,1)}, bf16[2,128,256]{2,1,0:...) custom-call(bf16[2,64,2048]{2,1,0:T(8,128)(2,1)} %feat.1, ...), custom_call_target="tpu_custom_call" | custom-call | tf_op jit(solution)/shard_map/pallas_call | solution.py:564
  183.7 5.9 %shard_map.138 = (f32[2048,256]{1,0:T(8,128)}, f32[2048,256]{1,0:T(8,128)}, f32[256,2048]{1,0:T(8,128)}, f32[256,128]{1,0:T(8,128)}, f32[128,256]{1,0:T(8,128)}) custom-call(bf16[2,4,128,512]{3,2,1,0:T(8,128)(2,1)} %bitcast.28, f32[2,128,1]{2,1,0:T(8,128)} %get-tuple-element.18.scale, bf16[2,4,128,512]{3,2,1,0:T(8,128)(2,1)} %bitcast.29, ...), custom_call_target="tpu_custom_call" | custom-call | tf_op jit(solution)/shard_map/pallas_call | solution.py:606

commit v3 on v2

--- a/solution.py
+++ b/solution.py
@@ -357,10 +357,13 @@
                     values = lines_of(slots, m, c, peers).astype(f32)
                     result = (row_scale * products[c] - values * weight).astype(bf16)
                     outgoing[m, c, peers] = result.reshape(group, slot, part_width)
+                    if experts == group:
+                        send_slots(3, m, c, back)
 
             in_groups(answer)
-            for c in range(PIECES):
-                send_slots(3, m, c, back)
+            if experts > group:
+                for c in range(PIECES):
+                    send_slots(3, m, c, back)
 
     def end_backward(m):
         @pl.when(sec > 0)
@@ -441,12 +444,25 @@
             serve_backward(m)
             end_backward(m)
 
-    def share_copy(peer, owner):
-        part = pl.ds(pl.multiple_of(peer * piece, piece), piece)
+    half = experts // 2
+    side, chip = lax.rem(me, 2), me // 2
+    sibling = me + 1 - 2 * side
+
+    def part_of(owner):
+        return pl.ds(pl.multiple_of(owner * piece, piece), piece)
+
+    def pair_copy(j, parity):
         return pltpu.make_async_remote_copy(
-            src_ref=low_all.at[:, :, part, :], dst_ref=parts.at[owner],
-            send_sem=p_send.at[peer], recv_sem=p_recv.at[owner],
-            device_id=(sec, peer), device_id_type=MESH,
+            src_ref=low_all.at[:, :, part_of(2 * j + parity), :], dst_ref=parts.at[j],
+            send_sem=p_send.at[j], recv_sem=p_recv.at[j],
+            device_id=(sec, sibling), device_id_type=MESH,
+        )
+
+    def share_copy(to, origin):
+        return pltpu.make_async_remote_copy(
+            src_ref=low_all.at[:, :, part_of(2 * to + side), :], dst_ref=parts.at[half + origin],
+            send_sem=p_send.at[half + to], recv_sem=p_recv.at[half + origin],
+            device_id=(sec, 2 * to + side), device_id_type=MESH,
         )
 
     def share_out(section):
@@ -473,22 +489,37 @@
 
         lax.fori_loop(0, sections, products, 0)
 
-        @pl.loop(1, experts)
-        def _(k):
-            share_copy(lax.rem(me + k, experts), me).start()
-
-    @pl.when(sec == last)
-    def _():
-        @pl.loop(1, experts)
-        def _(k):
-            peer = lax.rem(me + k, experts)
-            share_copy(peer, peer).wait_recv()
+        @pl.loop(1, half + 1)
+        def _(k):
+            pair_copy(lax.rem(chip + k, half), 1 - side).start()
+
+        @pl.loop(1, half + 1)
+        def _(k):
+            to = lax.rem(chip + k, half)
+            pair_copy(to, side).wait_recv()
+
+            def join(layer, carry):
+                own = low_all[layer, :, part_of(2 * to + side), :].astype(f32)
+                joined = own + parts[to, layer].astype(f32)
+                low_all[layer, :, part_of(2 * to + side), :] = joined.astype(bf16)
+                return carry
+
+            lax.fori_loop(0, sections, join, 0)
+
+            @pl.when(k < half)
+            def _():
+                share_copy(to, chip).start()
+
+        @pl.loop(1, half)
+        def _(k):
+            origin = lax.rem(chip + k, half)
+            share_copy(origin, origin).wait_recv()
 
         def total(layer, carry):
             def add(k, acc):
-                return acc + parts[lax.rem(me + k, experts), layer].astype(f32)
-
-            acc = lax.fori_loop(1, experts, add, low_all[layer, :, mine, :].astype(f32))
+                return acc + parts[half + lax.rem(chip + k, half), layer].astype(f32)
+
+            acc = lax.fori_loop(1, half, add, low_all[layer, :, mine, :].astype(f32))
             shares[layer] = acc.astype(bf16)
             return carry
 
@@ -504,9 +535,13 @@
         def _(section):
             share_out(section).wait_send()
 
-        @pl.loop(1, experts)
-        def _(k):
-            share_copy(lax.rem(me + k, experts), me).wait_send()
+        @pl.loop(1, half)
+        def _(k):
+            share_copy(lax.rem(chip + k, half), chip).wait_send()
+
+        @pl.loop(0, half)
+        def _(j):
+            pair_copy(j, 1 - side).wait_send()
 
     @pl.when(sec < last)
     def _():

time: 190 us -> 185 us (0.974)
  Pallas kernels: 189 us -> 183 us
    pallas_call x1, Pallas kernels: 183 us -> 177 us  [local(): pl.pallas_call(functools.partial(kernel, sections, experts, slot), out_sh...]
where the time goes in v3:
time: 185 us; the launch traced here: 184 us
  Pallas kernels  183 us (99%)
    pallas_call x1, Pallas kernels, local(): pl.pallas_call(functools.partial(kernel, sections, experts, slot), out_sh...  177 us
    pallas_call x1, Pallas kernels, local(): pl.pallas_call(products_kernel, grid=(PIECES,), out_shape=(jax.ShapeDtype...  5.93 us

profile of v3, /device:TPU:1, one launch (start us, length us, event | category | flops | bytes accessed | tf_op | source)
XLA Modules:
  0.0 184.2 jit_solution(4824393310978588396)
XLA Ops:
  0.6 177.5 %shard_map.137 = (bf16[2,4,8,16,512]{4,3,2,1,0:T(8,128)(2,1)}, f32[2,128,1]{2,1,0:T(8,128)}, bf16[2,4,8,16,512]{4,3,2,1,0:T(8,128)(2,1)}, bf16[2,128,256]{2,1,0:...) custom-call(bf16[2,64,2048]{2,1,0:T(8,128)(2,1)} %feat.1, ...), custom_call_target="tpu_custom_call" | custom-call | tf_op jit(solution)/shard_map/pallas_call | solution.py:599
  178.1 5.9 %shard_map.138 = (f32[2048,256]{1,0:T(8,128)}, f32[2048,256]{1,0:T(8,128)}, f32[256,2048]{1,0:T(8,128)}, f32[256,128]{1,0:T(8,128)}, f32[128,256]{1,0:T(8,128)}) custom-call(bf16[2,4,128,512]{3,2,1,0:T(8,128)(2,1)} %bitcast.28, f32[2,128,1]{2,1,0:T(8,128)} %get-tuple-element.18.scale, bf16[2,4,128,512]{3,2,1,0:T(8,128)(2,1)} %bitcast.29, ...), custom_call_target="tpu_custom_call" | custom-call | tf_op jit(solution)/shard_map/pallas_call | solution.py:641
